TPU v7x, 256 devices: a whole 4x4x8 slice. The times are simulated.
256 devices in a mesh: batch: 4 (over z_lo), pencil: 64 (over y, x, z_hi, core).
Axes of the slice: x: 4, y: 4, z: 8 (z_hi: 2, z_lo: 4; z = z_hi * 4 + z_lo), core: 2. Of those that a mesh axis runs over, the one named last changes fastest.
Arguments:
- state_field: float32 [8, 128, 32, 32, 128], P('batch', 'pencil'), may hold values from -6 to 6
- spectral_weight: float32 [128, 2, 32, 32, 16], P('pencil'), may hold values from -6 to 6
- local_weight: float32 [32, 32], replicated, may hold values from -1 to 1
- channel_bias: float32 [32], replicated, may hold values from -3 to 3
- cotangent: float32 [8, 128, 32, 32, 128], P('batch', 'pencil'), may hold values from -6 to 6
Outputs:
- layer_out: float32 [8, 128, 32, 32, 128], P('batch', 'pencil')
- grad_state: float32 [8, 128, 32, 32, 128], P('batch', 'pencil')
- grad_spectral: float32 [128, 2, 32, 32, 16], P('pencil')
- grad_local: float32 [32, 32], replicated
- grad_bias: float32 [32], replicated
All inputs are finite; a program needn't handle non-finite values.
Results may differ from a plain program's by a relative error of at most 0.00011.
Values sent between devices are 32-bit elements; how exact they have to be, the bound alone decides.
A program may use at most 128 MiB of HBM per device.

v0:
```python
import math
import types

import jax
import jax.numpy as jnp
import ml_dtypes
import numpy as np
from jax import lax
from jax.experimental import pallas as pl
from jax.experimental.pallas import tpu as pltpu
from jax.sharding import PartitionSpec as P

X, Y, Z, C = 128, 128, 32, 32
MX, MY, MZ = 16, 16, 8
PEERS, GROUPS = 64, 4
F32, BF16 = jnp.float32, jnp.bfloat16
gelu_scale = math.sqrt(2.0 / math.pi)
cubic_term = 0.044715
MESH = pl.DeviceIdType.MESH


def angles(points, kept_modes):
    order = np.arange(kept_modes)
    frequency = np.where(order < kept_modes // 2, order, points - kept_modes + order)
    phases = (np.arange(points)[:, None] * frequency[None, :]) % points
    theta = phases * (2.0 * np.pi / points)
    return np.cos(theta), np.sin(theta)


def halves(table):
    table = table.astype(np.float32)
    high = table.astype(ml_dtypes.bfloat16)
    low = (table - high.astype(np.float32)).astype(ml_dtypes.bfloat16)
    return high, low


def left(table):
    high, low = halves(table)
    return np.concatenate([high, low, high], axis=1)


def build_tables():
    cos_x, sin_x = angles(X, MX)
    cos_y, sin_y = angles(Y, MY)
    cos_z, sin_z = angles(Z, MZ)
    scaling = 1.0 / math.sqrt(X * Y * Z)
    zf = np.stack([cos_z.T, -sin_z.T], axis=1)
    zf = np.einsum("krz,cd->krcdz", zf, np.eye(8)).reshape(128, 256)
    xf = np.stack(
        [np.stack([cos_x.T, sin_x.T], 1), np.stack([-sin_x.T, cos_x.T], 1)], 1
    )
    xf = np.einsum("kabx,pq->kapqbx", xf, np.eye(2)).reshape(64, 512) * scaling
    cy = cos_y.reshape(64, 2, 16)
    sy = sin_y.reshape(64, 2, 16)
    yf = np.stack([np.stack([cy, sy], 0), np.stack([-sy, cy], 0)], 0)
    yf = np.einsum("abpyq,mn->ymaqpbn", yf, np.eye(2)).reshape(128, 256)
    xi = np.stack(
        [np.stack([cos_x.T, sin_x.T], 1), np.stack([-sin_x.T, cos_x.T], 1)], 0
    )
    xi = np.einsum("akbx,mn->maknbx", xi, np.eye(4)).reshape(128, 1024) * scaling
    xi_high, xi_low = halves(xi)
    return (
        left(zf),
        left(xf),
        left(yf),
        left(yf.T),
        np.concatenate([xi_high, xi_low, xi_high], axis=0),
        left(zf.T),
    )


RING = (0, 1, 2, 1)
FAR_FIRST = sorted(
    ((dy, dx) for dy in range(4) for dx in range(4)), key=lambda d: -RING[d[0]] - RING[d[1]]
)


def split(value):
    high = value.astype(BF16)
    return high, (value - high.astype(F32)).astype(BF16)


def rows_of(value):
    high, low = split(value)
    return jnp.concatenate([high, high, low], axis=0)


def lanes_of(value):
    high, low = split(value)
    return jnp.concatenate([high, high, low], axis=1)


def dot(a, b):
    return jnp.dot(a, b, preferred_element_type=F32)


def dot_nt(a, b):
    return lax.dot_general(a, b, (((1,), (1,)), ((), ())), preferred_element_type=F32)


def dot_tn(a, b):
    return lax.dot_general(a, b, (((0,), (0,)), ((), ())), preferred_element_type=F32)


def iota(shape, dim):
    return lax.broadcasted_iota(jnp.int32, shape, dim)


def roll(value, shift):
    shift = shift % value.shape[1]
    return value if shift == 0 else pltpu.roll(value, shift, 1)


def z_forward(r, block2, t, pair):
    res = dot(r.zf[...], rows_of(block2))
    order = (t % 2) * 2 + t // 2
    for half in range(2):
        row = order * 32 + (2 * pair + half) * 8
        for kz in range(8):
            for ri in range(2):
                k = kz * 2 + ri
                r.modes[kz // 2, pl.ds(row, 8), pl.ds(((kz % 2) * 2 + ri) * 128, 128)] = res[
                    k * 8 : k * 8 + 8, half * 128 : half * 128 + 128
                ]


def x_forward(r, send, dispatch):
    for kzp in range(4):
        res = dot_nt(r.xf[...], lanes_of(r.modes[kzp]))
        for kx in range(16):
            send[kx * 4 + kzp] = res[kx * 4 : kx * 4 + 4]
        for dy, dx in FAR_FIRST:
            dispatch(dy, dx, kzp)


def y_forward(r, recv):
    lane = iota((16, 128), 1)
    got = recv[...].reshape(256, 128)
    res = dot(r.yf[...], rows_of(got))
    res = res[0:64] + roll(res[64:128], 64)
    rows = []
    for b in range(2):
        total = jnp.zeros((16, 128), F32)
        for g in range(4):
            piece = roll(res[g * 16 : g * 16 + 16], (g - b) * 32)
            total = jnp.where(lane // 32 == g, piece, total)
        rows.append(total)
    return jnp.concatenate(rows, axis=0)


def y_inverse(r, value, send, my_y, dispatch):
    lane = iota((16, 128), 1)
    tops = []
    for g in range(4):
        first = roll(value[0:16], -g * 32)
        second = roll(value[16:32], (1 - g) * 32)
        tops.append(jnp.where(lane < 32, first, jnp.where(lane < 64, second, 0.0)))
    top = jnp.concatenate(tops, axis=0)
    both = jnp.concatenate([top, roll(top, 64)], axis=0)
    both = rows_of(both)
    for dy in (2, 1, 3, 0):
        to_y = (my_y + dy) % 4
        table = r.yi[pl.ds(pl.multiple_of(to_y * 64, 64), 64), :]
        res = dot(table, both)
        send[pl.ds(to_y * 16, 16)] = res.reshape(16, 4, 128)
        for dx in (2, 1, 3, 0):
            for to_z in range(4):
                dispatch(dy, dx, to_z)


def masked(parts, j):
    row_q = iota((32, 128), 0) % 16
    picks = [row_q == 2 * j, row_q == 2 * j + 1]

    def pick(part):
        wide = part.astype(F32)
        return jnp.concatenate(
            [jnp.where(p, wide, 0.0).astype(BF16) for p in picks], axis=1
        )

    return pick(parts[0]), pick(parts[1])


def x_inverse(r, recv):
    r.flat[...] = recv[...].reshape(256, 128)
    for g in range(2):
        pieces = []
        for k4 in range(4):
            kz = g * 4 + k4
            for ri in range(2):
                start = (kz // 2) * 4 + ri * 2 + kz % 2
                pieces.append(r.flat[pl.ds(start, 16, stride=16), :])
        block = jnp.concatenate(pieces, axis=0)
        turned = block.T
        r.spread[g] = dot(lanes_of(turned), r.xi[...])


def z_inverse(r, t, pair):
    order = (t % 2) * 2 + t // 2
    columns = []
    for half in range(2):
        row = order * 32 + (2 * pair + half) * 8
        tiles = []
        for k in range(16):
            tiles.append(r.spread[k // 8, pl.ds(row, 8), pl.ds((k % 8) * 128, 128)])
        columns.append(jnp.concatenate(tiles, axis=0))
    block = jnp.concatenate(columns, axis=1)
    return dot(r.zi[...], rows_of(block))


def channel_mix(table, src, dst, shift=None):
    for t in range(4):
        for pair in range(2):
            cols = []
            for half in range(2):
                zb = 2 * pair + half
                cols.append(src[t, :, pl.ds(zb * 8, 8), :].reshape(256, 128))
            res = dot(table[...], rows_of(jnp.concatenate(cols, axis=1)))
            for half in range(2):
                zb = 2 * pair + half
                part = res[:, half * 128 : half * 128 + 128].reshape(32, 8, 128)
                if shift is not None:
                    part = part + shift[...]
                dst[t, :, pl.ds(zb * 8, 8), :] = part


def pair_of(src, t, pair):
    return jnp.concatenate(
        [src[t, pl.ds((2 * pair + half) * 8, 8)].reshape(256, 128) for half in range(2)],
        axis=1,
    )


def state_cells(r, t):
    for pair in range(2):
        z_forward(r, pair_of(r.v, t, pair), t, pair)


def same_z():
    return iota((256, 256), 0) % 8 == iota((256, 256), 1) % 8


def pointwise_tables(r):
    expand = (iota((256, 32), 0) // 8 == iota((256, 32), 1)).astype(F32).astype(BF16)
    same = same_z()
    lw_high, lw_low = split(r.lw[...])
    for i, part_of in enumerate((lw_high, lw_low, lw_high)):
        once = dot_nt(expand, part_of).astype(BF16)
        r.kron_f[:, pl.ds(i * 256, 256)] = jnp.where(same, dot_nt(once, expand), 0.0).astype(BF16)
        once = dot(expand, part_of).astype(BF16)
        r.kron_b[:, pl.ds(i * 256, 256)] = jnp.where(same, dot_nt(once, expand), 0.0).astype(BF16)


    for o in range(32):
        r.shift[o] = jnp.full((8, 128), r.bias[o], F32)


def mode_tables(r):
    zeros = jnp.zeros((32, 32), F32)
    for q in range(16):
        rows = []
        for m in range(2):
            real = r.w[pl.ds((m * 2 + 0) * 512 + q, 32, stride=16), :]
            imag = r.w[pl.ds((m * 2 + 1) * 512 + q, 32, stride=16), :]
            for ri, pieces in enumerate(((real, imag), (-imag, real))):
                pieces = list(pieces)
                both = pieces + [zeros, zeros] if m == 0 else [zeros, zeros] + pieces
                rows.append(jnp.concatenate(both, axis=1))
        block = jnp.concatenate(rows, axis=0)
        r.bw_high[q], r.bw_low[q] = split(block)
        r.bwt_high[q], r.bwt_low[q] = split(block.T)


def all_modes(value, right_high, right_low):
    parts = split(value)
    total = jnp.zeros((32, 128), F32)
    for j in range(8):
        high, low = masked(parts, j)
        r_high = right_high[2 * j : 2 * j + 2].reshape(256, 128)
        r_low = right_low[2 * j : 2 * j + 2].reshape(256, 128)
        total = total + dot(
            jnp.concatenate([high, high, low], axis=1),
            jnp.concatenate([r_high, r_low, r_high], axis=0),
        )
    return total


def mix(r, own, my_y, dispatch):
    spectrum = y_forward(r, r.recv0)
    r.s_all[own, :] = spectrum
    mixed = all_modes(spectrum, r.bw_high, r.bw_low)
    y_inverse(r, mixed, r.send1, my_y, dispatch)


def mix_adjoint(r, own, my_y, dispatch, share):
    grad_modes = y_forward(r, r.recv2)
    r.g_all[own, :] = grad_modes
    share()
    back = all_modes(grad_modes, r.bwt_high, r.bwt_low)
    y_inverse(r, back, r.send3, my_y, dispatch)


def cells(r, t):
    for pair in range(2):
        field = z_inverse(r, t, pair)
        columns = []
        for half in range(2):
            pieces = []
            for o8 in range(8):
                o = (2 * pair + half) * 8 + o8
                pre = field[o8 * 32 : o8 * 32 + 32, half * 128 : half * 128 + 128] + r.loc[t, o]
                square = pre * pre
                bent = jnp.tanh(pre * (gelu_scale + (gelu_scale * cubic_term) * square))
                half_up = 0.5 + 0.5 * bent
                r.lay[t, o] = pre * half_up
                rise = (0.5 * gelu_scale) + (1.5 * gelu_scale * cubic_term) * square
                slope = half_up + (pre * rise) * (1.0 - bent * bent)
                grad = r.cot[t, o] * slope
                r.gp[t, o] = grad
                pieces.append(grad)
            columns.append(jnp.concatenate(pieces, axis=0))
        z_forward(r, jnp.concatenate(columns, axis=1), t, pair)


def point_sums(r):
    same = same_z()
    r.acc[...] = jnp.zeros((256, 256), F32)
    for t in range(4):
        for pair in range(2):
            a_cols, b_cols = [], []
            for half in range(2):
                zb = 2 * pair + half
                a_cols.append(r.v[t, :, pl.ds(zb * 8, 8), :].reshape(256, 128))
                b_cols.append(r.gp[t, :, pl.ds(zb * 8, 8), :].reshape(256, 128))
            a_high, a_low = split(jnp.concatenate(a_cols, axis=1))
            b_high, b_low = split(jnp.concatenate(b_cols, axis=1))
            r.acc[...] += dot_nt(
                jnp.concatenate([a_high, a_high, a_low], axis=1),
                jnp.concatenate([b_high, b_low, b_high], axis=1),
            )
    folded = jnp.sum(jnp.where(same, r.acc[...], 0.0).reshape(32, 8, 256), axis=1)
    pick = (iota((256, 128), 0) // 8 == iota((256, 128), 1)).astype(F32).astype(BF16)
    fold_high, fold_low = split(folded)
    pointwise = dot(
        jnp.concatenate([fold_high, fold_low], axis=1), jnp.concatenate([pick, pick], axis=0)
    )
    dense = pointwise[0:8]
    for k in range(1, 4):
        dense = dense + roll(pointwise[8 * k : 8 * k + 8], 32 * k)
    sums = jnp.sum(r.gp[0], axis=1)
    for t in range(1, 4):
        sums = sums + jnp.sum(r.gp[t], axis=1)
    sum_high, sum_low = split(sums)
    ones = jnp.ones((8, 256), BF16)
    bias_row = dot_nt(
        ones,
        jnp.concatenate(
            [jnp.concatenate([sum_high, sum_low], axis=1), jnp.zeros((96, 256), BF16)], axis=0
        ),
    )
    for i in range(8):
        r.part1[i] = dense[i : i + 1]
        r.part1[8 + i] = bias_row[i : i + 1]


def weight_gradient(r):
    lane8 = iota((8, 128), 1)
    sign = jnp.where(lane8 // 32 % 2 == 0, 1.0, -1.0)
    low_half = lane8 < 64
    for q in range(16):
        s_q = r.s_all[pl.ds(q, 8, stride=16), :]
        g_q = r.g_all[pl.ds(q, 8, stride=16), :]
        first = s_q * sign
        second = jnp.where(lane8 // 32 % 2 == 0, roll(s_q, -32), roll(s_q, 32))
        left_rows = jnp.concatenate(
            [
                jnp.where(low_half, first, 0.0),
                jnp.where(low_half, second, 0.0),
                jnp.where(low_half, 0.0, first),
                jnp.where(low_half, 0.0, second),
            ],
            axis=0,
        )
        right_rows = jnp.concatenate([roll(g_q, -32 * g) for g in range(4)], axis=0)
        l_high, l_low = split(left_rows)
        r_high, r_low = split(right_rows)
        res = dot_tn(
            jnp.concatenate([l_high, l_high, l_low], axis=0),
            jnp.concatenate([r_high, r_low, r_high], axis=0),
        )
        r.gspec[pl.ds(q, 128, stride=16), :] = res[:, 0:32]


def final_cells(r, t):
    for pair in range(2):
        field = z_inverse(r, t, pair)
        for half in range(2):
            ob = 2 * pair + half
            r.res[t, pl.ds(ob * 8, 8)] = r.loc[t, pl.ds(ob * 8, 8)] + field[
                :, half * 128 : half * 128 + 128
            ].reshape(8, 32, 128)


CELLS, SLOTS = (4, 32, 32, 128), (64, 4, 128)
IN_NAMES = "v w lw bias cot zf xf yf yi xi zi".split()
OUT_SHAPES = dict(
    lay=(CELLS, F32), loc=(CELLS, F32), gspec=((2048, 32), F32), recv3=(SLOTS, F32),
    total=((16, 1, 128), F32), xi=((384, 1024), BF16), zi=((256, 384), BF16),
)
SCRATCH = dict(
    v=(CELLS, F32), w=((2048, 32), F32), lw=((32, 32), F32), cot=(CELLS, F32),
    zf=((128, 768), BF16), xf=((64, 1536), BF16), yf=((128, 768), BF16), yi=((256, 384), BF16),
    modes=((4, 128, 512), F32), gp=(CELLS, F32),
    bw_high=((16, 128, 128), BF16), bw_low=((16, 128, 128), BF16),
    bwt_high=((16, 128, 128), BF16), bwt_low=((16, 128, 128), BF16),
    kron_f=((256, 768), BF16), kron_b=((256, 768), BF16),
    flat=((256, 128), F32), spread=((2, 128, 1024), F32),
    s_all=((128, 128), F32), g_all=((128, 128), F32), acc=((256, 256), F32),
    part1=((16, 1, 128), F32), stage1=((16, 1, 128), F32),
    part2=((1, 128), F32), stage2=((16, 1, 128), F32), part3=((1, 128), F32),
    shift=((32, 8, 128), F32),
    send0=(SLOTS, F32), send1=(SLOTS, F32), send2=(SLOTS, F32), send3=(SLOTS, F32),
    recv0=(SLOTS, F32), recv1=(SLOTS, F32), recv2=(SLOTS, F32),
)
SEMAPHORES = dict(in_sem=16, send_sem=6, recv_sem=6, small_send=3, small_recv=3)


def kernel(*refs):
    names = [n + "_hbm" for n in IN_NAMES]
    names += list(OUT_SHAPES) + list(SCRATCH) + ["bias"] + list(SEMAPHORES)
    r = types.SimpleNamespace(**dict(zip(names, refs, strict=True)))
    me = lax.axis_index("pencil")
    group = lax.axis_index("batch")
    my_y, my_x, my_z = me // 16, me // 4 % 4, me % 4
    across = (group + 2) % GROUPS

    def peer_of(dy, dx, to_z):
        return (my_y + dy) % 4 * 16 + (my_x + dx) % 4 * 4 + to_z

    barrier = pltpu.get_barrier_semaphore()
    for dy, dx in FAR_FIRST:
        for to_z in range(4):
            pl.semaphore_signal(
                barrier, inc=1, device_id=(across, peer_of(dy, dx, to_z)), device_id_type=MESH
            )
    greetings = PEERS
    around = []
    for dg in range(4):
        for dz in range(4):
            if dg == 0 and dz == 0:
                continue
            near = ((group + dg) % GROUPS, me - my_z + (my_z + dz) % 4)
            around.append(near)
            if dg != 2:
                greetings += 1
                pl.semaphore_signal(barrier, inc=1, device_id=near, device_id_type=MESH)

    loads = {}

    def load(name, src, dst):
        loads[name] = pltpu.make_async_copy(src, dst, r.in_sem.at[len(loads)])
        loads[name].start()

    load("zf", r.zf_hbm, r.zf)
    for t in range(4):
        load("v%d" % t, r.v_hbm.at[t], r.v.at[t])
    for name in "xf bias lw w yf yi xi zi cot".split():
        load(name, getattr(r, name + "_hbm"), getattr(r, name))

    def send_to(send, recv, index):
        def dispatch(dy, dx, to_z):
            peer = peer_of(dy, dx, to_z)
            pltpu.make_async_remote_copy(
                src_ref=send.at[peer],
                dst_ref=recv.at[me],
                send_sem=r.send_sem.at[index],
                recv_sem=r.recv_sem.at[index],
                device_id=(across, peer),
                device_id_type=MESH,
            ).start()

        return dispatch

    def await_bytes(ref, sem):
        pltpu.make_async_copy(ref, ref, sem).wait()

    own = pl.ds(pl.multiple_of(group * 32, 32), 32)

    def share(buffer, index):
        for dg in (2, 1, 3):
            pltpu.make_async_remote_copy(
                src_ref=buffer.at[own],
                dst_ref=buffer.at[own],
                send_sem=r.send_sem.at[index],
                recv_sem=r.recv_sem.at[index],
                device_id=((group + dg) % GROUPS, me),
                device_id_type=MESH,
            ).start()

    spot = group * 4 + my_z
    fifteen = pl.ds(0, 15)

    loads["zf"].wait()
    for t in range(4):
        loads["v%d" % t].wait()
        state_cells(r, t)
    loads["xf"].wait()
    pl.semaphore_wait(barrier, greetings)
    x_forward(r, r.send0, send_to(r.send0, r.recv0, 0))

    loads["lw"].wait()
    loads["bias"].wait()
    pointwise_tables(r)
    loads["w"].wait()
    mode_tables(r)
    channel_mix(r.kron_f, r.v, r.loc, r.shift)

    loads["yf"].wait()
    loads["yi"].wait()
    await_bytes(r.recv0, r.recv_sem.at[0])
    mix(r, own, my_y, send_to(r.send1, r.recv1, 1))

    loads["xi"].wait()
    loads["zi"].wait()
    loads["cot"].wait()
    await_bytes(r.recv1, r.recv_sem.at[1])
    share(r.s_all, 4)
    x_inverse(r, r.recv1)
    for t in range(4):
        cells(r, t)
    x_forward(r, r.send2, send_to(r.send2, r.recv2, 2))

    point_sums(r)
    for i, (to_group, to_peer) in enumerate(around):
        pltpu.make_async_remote_copy(
            src_ref=r.part1.at[to_group * 4 + to_peer % 4],
            dst_ref=r.stage1.at[spot],
            send_sem=r.small_send.at[0],
            recv_sem=r.small_recv.at[0],
            device_id=(to_group, to_peer),
            device_id_type=MESH,
        ).start()
    r.stage1[spot] = r.part1[spot]
    channel_mix(r.kron_b, r.gp, r.loc)

    await_bytes(r.stage1.at[fifteen], r.small_recv.at[0])
    r.part2[...] = jnp.sum(r.stage1[...], axis=0)
    for dy, dx in FAR_FIRST:
        pltpu.make_async_remote_copy(
            src_ref=r.part2,
            dst_ref=r.stage2.at[me // 4],
            send_sem=r.small_send.at[1],
            recv_sem=r.small_recv.at[1],
            device_id=(across, peer_of(dy, dx, my_z)),
            device_id_type=MESH,
        ).start()
    await_bytes(r.recv2, r.recv_sem.at[2])
    mix_adjoint(r, own, my_y, send_to(r.send3, r.recv3, 3), lambda: share(r.g_all, 5))

    await_bytes(r.stage2, r.small_recv.at[1])
    r.part3[...] = jnp.sum(r.stage2[...], axis=0) * (1.0 / math.sqrt(8 * X * Y * Z))
    for to_group, to_peer in around:
        pltpu.make_async_remote_copy(
            src_ref=r.part3,
            dst_ref=r.total.at[across * 4 + my_z],
            send_sem=r.small_send.at[2],
            recv_sem=r.small_recv.at[2],
            device_id=(to_group, to_peer),
            device_id_type=MESH,
        ).start()
    r.total[across * 4 + my_z] = r.part3[...]
    for buffer, index in ((r.s_all, 4), (r.g_all, 5)):
        await_bytes(buffer.at[pl.ds(0, 96)], r.recv_sem.at[index])
    weight_gradient(r)

    for index, buffer in enumerate((r.send0, r.send1, r.send2, r.send3)):
        await_bytes(buffer, r.send_sem.at[index])
    for index, buffer in ((4, r.s_all), (5, r.g_all)):
        await_bytes(buffer.at[pl.ds(0, 96)], r.send_sem.at[index])
    await_bytes(r.stage1.at[fifteen], r.small_send.at[0])
    await_bytes(r.stage2, r.small_send.at[1])
    await_bytes(r.total.at[fifteen], r.small_send.at[2])
    await_bytes(r.total.at[fifteen], r.small_recv.at[2])
    await_bytes(r.recv3, r.recv_sem.at[3])


TAIL_SCRATCH = dict(
    flat=((256, 128), F32), spread=((2, 128, 1024), F32), res=(CELLS, F32),
)


def tail(*refs):
    names = list(OUT_SHAPES) + "layer_out grad_state grad_spectral grad_local grad_bias".split()
    names += list(TAIL_SCRATCH) + ["sem"]
    r = types.SimpleNamespace(**dict(zip(names, refs, strict=True)))
    copies = []

    def copy(src, dst):
        copies.append(pltpu.make_async_copy(src, dst, r.sem.at[len(copies)]))
        copies[-1].start()

    copy(r.lay, r.layer_out)
    copy(r.gspec, r.grad_spectral)
    total = r.total[...].reshape(16, 128)
    for k in range(4):
        r.grad_local[pl.ds(8 * k, 8), :] = roll(total[0:8], -32 * k)[:, 0:32]
    r.grad_bias[...] = total[8:9, 0:32]
    x_inverse(r, r.recv3)
    for t in range(4):
        final_cells(r, t)
        copy(r.res.at[t], r.grad_state.at[t])
    for pending in copies:
        pending.wait()


def vmem(array):
    return pltpu.with_memory_space_constraint(array, pltpu.VMEM)


def hbm(array):
    return pltpu.with_memory_space_constraint(array, pltpu.HBM)


def shards(state_field, spectral_weight, local_weight, channel_bias, cotangent):
    tables = [hbm(jnp.asarray(t)) for t in build_tables()]
    in_hbm = pl.BlockSpec(memory_space=pltpu.HBM)
    in_vmem = pl.BlockSpec(memory_space=pltpu.VMEM)
    held = pl.pallas_call(
        kernel,
        out_shape=tuple(pltpu.VMEM(*s) for s in OUT_SHAPES.values()),
        in_specs=[in_hbm] * len(IN_NAMES),
        out_specs=(in_vmem,) * len(OUT_SHAPES),
        scratch_shapes=[pltpu.VMEM(*s) for s in SCRATCH.values()]
        + [pltpu.SMEM((32,), F32)]
        + [pltpu.SemaphoreType.DMA((n,)) for n in SEMAPHORES.values()],
        compiler_params=pltpu.CompilerParams(
            collective_id=0, has_side_effects=True, vmem_limit_bytes=40 * 1024 * 1024
        ),
        name="fno_layer",
    )(
        hbm(state_field.reshape(CELLS)),
        hbm(jnp.swapaxes(spectral_weight, 3, 4).reshape(2048, 32)),
        hbm(local_weight),
        hbm(channel_bias),
        hbm(cotangent.reshape(CELLS)),
        *tables,
    )
    out = pl.pallas_call(
        tail,
        out_shape=(
            jax.ShapeDtypeStruct(CELLS, F32),
            jax.ShapeDtypeStruct(CELLS, F32),
            jax.ShapeDtypeStruct((2048, 32), F32),
            jax.ShapeDtypeStruct((32, 32), F32),
            jax.ShapeDtypeStruct((1, 32), F32),
        ),
        in_specs=[in_vmem] * len(OUT_SHAPES),
        out_specs=(in_hbm, in_hbm, in_hbm, in_vmem, in_vmem),
        scratch_shapes=[pltpu.VMEM(*s) for s in TAIL_SCRATCH.values()]
        + [pltpu.SemaphoreType.DMA((6,))],
        compiler_params=pltpu.CompilerParams(vmem_limit_bytes=24 * 1024 * 1024),
        name="fno_tail",
    )(*[vmem(h) for h in held])
    layer_out, grad_state, grad_spectral, grad_local, grad_bias = out
    return (
        layer_out.reshape(state_field.shape),
        grad_state.reshape(state_field.shape),
        jnp.swapaxes(grad_spectral.reshape(2, 2, 32, 16, 32), 3, 4),
        grad_local,
        grad_bias.reshape(32),
    )


def solution(mesh):
    cells = P("batch", "pencil", None, None, None)
    modes = P("pencil", None, None, None, None)
    return jax.shard_map(
        shards,
        mesh=mesh,
        in_specs=(cells, modes, P(), P(), cells),
        out_specs=(cells, cells, modes, P(), P()),
        check_vma=False,
    )
```

profile of v0, /device:TPU:1, one launch (start us, length us, event | category | flops | bytes accessed | tf_op | source)
XLA Modules:
  0.0 54.5 jit_solution(8835778143619772259)
XLA Ops:
  0.6 50.8 %fno_layer.1 = (f32[4,32,32,128]{3,2,1,0:T(8,128)S(1)}, f32[4,32,32,128]{3,2,1,0:T(8,128)S(1)}, f32[2048,32]{1,0:T(8,128)S(1)}, f32[64,4,128]{2,1,0:T(4,128)S(1)...) custom-call(f32[4,32,32,128]{3,2,1,0:T(8,128)} %bitcast.11, ...), custom_call_target="tpu_custom_call" | custom-call | tf_op jit(solution)/shard_map/fno_layer/pallas_call | solution.py:628
  51.4 3.1 %fno_tail.1 = (f32[4,32,32,128]{3,2,1,0:T(8,128)}, f32[4,32,32,128]{3,2,1,0:T(8,128)}, f32[2048,32]{1,0:T(8,128)}, f32[32,32]{1,0:T(8,128)}, f32[1,32]{1,0:T(1,128)}) custom-call(f32[4,32,32,128]{3,2,1,0:T(8,128)S(1)} %get-tuple-element.17.refs_0_, f32[4,32,32,128]{3,2,1,0:T(8,128)S(1)} %get-tuple-element.18.refs_1_, ...), custom_call_target="tpu_custom_call" | custom-call | tf_op jit(solution)/shard_map/fno_tail/pallas_call | solution.py:648
where the time goes:
time: 54.6 us; the launch traced here: 54.5 us
  Pallas kernels  53.9 us (99%)
  between operations  0.64 us (1%)
    pallas_call x1, Pallas kernels, shards(): pl.pallas_call(kernel, out_shape=tuple((pltpu.VMEM(*s) for s in OUT_SHAPE...  50.8 us
    pallas_call x1, Pallas kernels, shards(): pl.pallas_call(tail, out_shape=(jax.ShapeDtypeStruct(CELLS, F32), jax.Sha...  3.11 us

commit v1 on v0

--- a/solution.py
+++ b/solution.py
@@ -63,12 +63,13 @@
         left(zf),
         left(xf),
         left(yf),
-        left(yf.T),
+        left(yf.T.reshape(16, 4, 4, 128).swapaxes(0, 1).reshape(256, 128)),
         np.concatenate([xi_high, xi_low, xi_high], axis=0),
         left(zf.T),
     )
 
 
+Z_ORDER = (0, 2, 1, 3)
 RING = (0, 1, 2, 1)
 FAR_FIRST = sorted(
     ((dy, dx) for dy in range(4) for dx in range(4)), key=lambda d: -RING[d[0]] - RING[d[1]]
@@ -125,12 +126,10 @@
 
 
 def x_forward(r, send, dispatch):
-    for kzp in range(4):
+    for kzp in Z_ORDER:
         res = dot_nt(r.xf[...], lanes_of(r.modes[kzp]))
-        for kx in range(16):
-            send[kx * 4 + kzp] = res[kx * 4 : kx * 4 + 4]
-        for dy, dx in FAR_FIRST:
-            dispatch(dy, dx, kzp)
+        send[kzp * 16 : kzp * 16 + 16] = res.reshape(16, 4, 128)
+        dispatch(kzp)
 
 
 def y_forward(r, recv):
@@ -148,7 +147,7 @@
     return jnp.concatenate(rows, axis=0)
 
 
-def y_inverse(r, value, send, my_y, dispatch):
+def y_inverse(r, value, send, dispatch):
     lane = iota((16, 128), 1)
     tops = []
     for g in range(4):
@@ -158,14 +157,10 @@
     top = jnp.concatenate(tops, axis=0)
     both = jnp.concatenate([top, roll(top, 64)], axis=0)
     both = rows_of(both)
-    for dy in (2, 1, 3, 0):
-        to_y = (my_y + dy) % 4
-        table = r.yi[pl.ds(pl.multiple_of(to_y * 64, 64), 64), :]
-        res = dot(table, both)
-        send[pl.ds(to_y * 16, 16)] = res.reshape(16, 4, 128)
-        for dx in (2, 1, 3, 0):
-            for to_z in range(4):
-                dispatch(dy, dx, to_z)
+    for to_z in Z_ORDER:
+        res = dot(r.yi[to_z * 64 : to_z * 64 + 64, :], both)
+        send[to_z * 16 : to_z * 16 + 16] = res.reshape(16, 4, 128)
+        dispatch(to_z)
 
 
 def masked(parts, j):
@@ -231,9 +226,9 @@
     )
 
 
-def state_cells(r, t):
+def field_modes(r, field, t):
     for pair in range(2):
-        z_forward(r, pair_of(r.v, t, pair), t, pair)
+        z_forward(r, pair_of(field, t, pair), t, pair)
 
 
 def same_z():
@@ -285,27 +280,24 @@
     return total
 
 
-def mix(r, own, my_y, dispatch):
+def mix(r, own, dispatch):
     spectrum = y_forward(r, r.recv0)
     r.s_all[own, :] = spectrum
     mixed = all_modes(spectrum, r.bw_high, r.bw_low)
-    y_inverse(r, mixed, r.send1, my_y, dispatch)
-
-
-def mix_adjoint(r, own, my_y, dispatch, share):
+    y_inverse(r, mixed, r.send1, dispatch)
+
+
+def mix_adjoint(r, own, dispatch):
     grad_modes = y_forward(r, r.recv2)
     r.g_all[own, :] = grad_modes
-    share()
     back = all_modes(grad_modes, r.bwt_high, r.bwt_low)
-    y_inverse(r, back, r.send3, my_y, dispatch)
+    y_inverse(r, back, r.send3, dispatch)
 
 
 def cells(r, t):
     for pair in range(2):
         field = z_inverse(r, t, pair)
-        columns = []
         for half in range(2):
-            pieces = []
             for o8 in range(8):
                 o = (2 * pair + half) * 8 + o8
                 pre = field[o8 * 32 : o8 * 32 + 32, half * 128 : half * 128 + 128] + r.loc[t, o]
@@ -317,9 +309,6 @@
                 slope = half_up + (pre * rise) * (1.0 - bent * bent)
                 grad = r.cot[t, o] * slope
                 r.gp[t, o] = grad
-                pieces.append(grad)
-            columns.append(jnp.concatenate(pieces, axis=0))
-        z_forward(r, jnp.concatenate(columns, axis=1), t, pair)
 
 
 def point_sums(r):
@@ -402,7 +391,7 @@
 
 
 CELLS, SLOTS = (4, 32, 32, 128), (64, 4, 128)
-IN_NAMES = "v w lw bias cot zf xf yf yi xi zi".split()
+IN_NAMES = ["v", "w", "lw", "bias", "cot", "zf", "xf", "yf", "yi", "xi", "zi"]
 OUT_SHAPES = dict(
     lay=(CELLS, F32), loc=(CELLS, F32), gspec=((2048, 32), F32), recv3=(SLOTS, F32),
     total=((16, 1, 128), F32), xi=((384, 1024), BF16), zi=((256, 384), BF16),
@@ -455,6 +444,12 @@
                 greetings += 1
                 pl.semaphore_signal(barrier, inc=1, device_id=near, device_id_type=MESH)
 
+    for dy, dx in FAR_FIRST[:-1]:
+        greetings += 1
+        pl.semaphore_signal(
+            barrier, inc=1, device_id=(group, peer_of(dy, dx, my_z)), device_id_type=MESH
+        )
+
     loads = {}
 
     def load(name, src, dst):
@@ -464,20 +459,21 @@
     load("zf", r.zf_hbm, r.zf)
     for t in range(4):
         load("v%d" % t, r.v_hbm.at[t], r.v.at[t])
-    for name in "xf bias lw w yf yi xi zi cot".split():
+    for name in ("xf", "bias", "lw", "w", "yf", "yi", "xi", "zi", "cot"):
         load(name, getattr(r, name + "_hbm"), getattr(r, name))
 
     def send_to(send, recv, index):
-        def dispatch(dy, dx, to_z):
-            peer = peer_of(dy, dx, to_z)
-            pltpu.make_async_remote_copy(
-                src_ref=send.at[peer],
-                dst_ref=recv.at[me],
-                send_sem=r.send_sem.at[index],
-                recv_sem=r.recv_sem.at[index],
-                device_id=(across, peer),
-                device_id_type=MESH,
-            ).start()
+        def dispatch(to_z):
+            for dy, dx in FAR_FIRST:
+                peer = peer_of(dy, dx, to_z)
+                pltpu.make_async_remote_copy(
+                    src_ref=send.at[to_z * 16 + peer // 4],
+                    dst_ref=recv.at[me],
+                    send_sem=r.send_sem.at[index],
+                    recv_sem=r.recv_sem.at[index],
+                    device_id=(across, peer),
+                    device_id_type=MESH,
+                ).start()
 
         return dispatch
 
@@ -503,10 +499,12 @@
     loads["zf"].wait()
     for t in range(4):
         loads["v%d" % t].wait()
-        state_cells(r, t)
+        field_modes(r, r.v, t)
     loads["xf"].wait()
+    x_forward(r, r.send0, lambda to_z: None)
     pl.semaphore_wait(barrier, greetings)
-    x_forward(r, r.send0, send_to(r.send0, r.recv0, 0))
+    for to_z in Z_ORDER:
+        send_to(r.send0, r.recv0, 0)(to_z)
 
     loads["lw"].wait()
     loads["bias"].wait()
@@ -518,7 +516,7 @@
     loads["yf"].wait()
     loads["yi"].wait()
     await_bytes(r.recv0, r.recv_sem.at[0])
-    mix(r, own, my_y, send_to(r.send1, r.recv1, 1))
+    mix(r, own, send_to(r.send1, r.recv1, 1))
 
     loads["xi"].wait()
     loads["zi"].wait()
@@ -528,6 +526,8 @@
     x_inverse(r, r.recv1)
     for t in range(4):
         cells(r, t)
+    for t in range(4):
+        field_modes(r, r.gp, t)
     x_forward(r, r.send2, send_to(r.send2, r.recv2, 2))
 
     point_sums(r)
@@ -545,30 +545,32 @@
 
     await_bytes(r.stage1.at[fifteen], r.small_recv.at[0])
     r.part2[...] = jnp.sum(r.stage1[...], axis=0)
-    for dy, dx in FAR_FIRST:
+    for dy, dx in FAR_FIRST[:-1]:
         pltpu.make_async_remote_copy(
             src_ref=r.part2,
             dst_ref=r.stage2.at[me // 4],
             send_sem=r.small_send.at[1],
             recv_sem=r.small_recv.at[1],
-            device_id=(across, peer_of(dy, dx, my_z)),
+            device_id=(group, peer_of(dy, dx, my_z)),
             device_id_type=MESH,
         ).start()
+    r.stage2[me // 4] = r.part2[...]
     await_bytes(r.recv2, r.recv_sem.at[2])
-    mix_adjoint(r, own, my_y, send_to(r.send3, r.recv3, 3), lambda: share(r.g_all, 5))
-
-    await_bytes(r.stage2, r.small_recv.at[1])
+    mix_adjoint(r, own, send_to(r.send3, r.recv3, 3))
+    share(r.g_all, 5)
+
+    await_bytes(r.stage2.at[fifteen], r.small_recv.at[1])
     r.part3[...] = jnp.sum(r.stage2[...], axis=0) * (1.0 / math.sqrt(8 * X * Y * Z))
     for to_group, to_peer in around:
         pltpu.make_async_remote_copy(
             src_ref=r.part3,
-            dst_ref=r.total.at[across * 4 + my_z],
+            dst_ref=r.total.at[spot],
             send_sem=r.small_send.at[2],
             recv_sem=r.small_recv.at[2],
             device_id=(to_group, to_peer),
             device_id_type=MESH,
         ).start()
-    r.total[across * 4 + my_z] = r.part3[...]
+    r.total[spot] = r.part3[...]
     for buffer, index in ((r.s_all, 4), (r.g_all, 5)):
         await_bytes(buffer.at[pl.ds(0, 96)], r.recv_sem.at[index])
     weight_gradient(r)
@@ -578,7 +580,7 @@
     for index, buffer in ((4, r.s_all), (5, r.g_all)):
         await_bytes(buffer.at[pl.ds(0, 96)], r.send_sem.at[index])
     await_bytes(r.stage1.at[fifteen], r.small_send.at[0])
-    await_bytes(r.stage2, r.small_send.at[1])
+    await_bytes(r.stage2.at[fifteen], r.small_send.at[1])
     await_bytes(r.total.at[fifteen], r.small_send.at[2])
     await_bytes(r.total.at[fifteen], r.small_recv.at[2])
     await_bytes(r.recv3, r.recv_sem.at[3])
@@ -590,7 +592,7 @@
 
 
 def tail(*refs):
-    names = list(OUT_SHAPES) + "layer_out grad_state grad_spectral grad_local grad_bias".split()
+    names = list(OUT_SHAPES) + ["layer_out", "grad_state", "grad_spectral", "grad_local", "grad_bias"]
     names += list(TAIL_SCRATCH) + ["sem"]
     r = types.SimpleNamespace(**dict(zip(names, refs, strict=True)))
     copies = []

time: 54.6 us -> 50.9 us (0.932)
  Pallas kernels: 53.9 us -> 50.2 us
    pallas_call x1, Pallas kernels: 50.8 us -> 47.1 us  [shards(): pl.pallas_call(kernel, out_shape=tuple((pltpu.VMEM(*s) for s in OUT_SHAPE...]
where the time goes in v1:
time: 50.9 us; the launch traced here: 50.8 us
  Pallas kernels  50.2 us (99%)
  between operations  0.64 us (1%)
    pallas_call x1, Pallas kernels, shards(): pl.pallas_call(kernel, out_shape=tuple((pltpu.VMEM(*s) for s in OUT_SHAPE...  47.1 us
    pallas_call x1, Pallas kernels, shards(): pl.pallas_call(tail, out_shape=(jax.ShapeDtypeStruct(CELLS, F32), jax.Sha...  3.11 us

profile of v1, /device:TPU:1, one launch (start us, length us, event | category | flops | bytes accessed | tf_op | source)
XLA Modules:
  0.0 50.8 jit_solution(760846519909968070)
XLA Ops:
  0.6 47.1 %fno_layer.1 = (f32[4,32,32,128]{3,2,1,0:T(8,128)S(1)}, f32[4,32,32,128]{3,2,1,0:T(8,128)S(1)}, f32[2048,32]{1,0:T(8,128)S(1)}, f32[64,4,128]{2,1,0:T(4,128)S(1)...) custom-call(f32[4,32,32,128]{3,2,1,0:T(8,128)} %bitcast.11, ...), custom_call_target="tpu_custom_call" | custom-call | tf_op jit(solution)/shard_map/fno_layer/pallas_call | solution.py:630
  47.7 3.1 %fno_tail.1 = (f32[4,32,32,128]{3,2,1,0:T(8,128)}, f32[4,32,32,128]{3,2,1,0:T(8,128)}, f32[2048,32]{1,0:T(8,128)}, f32[32,32]{1,0:T(8,128)}, f32[1,32]{1,0:T(1,128)}) custom-call(f32[4,32,32,128]{3,2,1,0:T(8,128)S(1)} %get-tuple-element.17.refs_0_, f32[4,32,32,128]{3,2,1,0:T(8,128)S(1)} %get-tuple-element.18.refs_1_, ...), custom_call_target="tpu_custom_call" | custom-call | tf_op jit(solution)/shard_map/fno_tail/pallas_call | solution.py:650

commit v2 on v1

--- a/solution.py
+++ b/solution.py
@@ -268,16 +268,13 @@
 
 def all_modes(value, right_high, right_low):
     parts = split(value)
-    total = jnp.zeros((32, 128), F32)
-    for j in range(8):
-        high, low = masked(parts, j)
-        r_high = right_high[2 * j : 2 * j + 2].reshape(256, 128)
-        r_low = right_low[2 * j : 2 * j + 2].reshape(256, 128)
-        total = total + dot(
-            jnp.concatenate([high, high, low], axis=1),
-            jnp.concatenate([r_high, r_low, r_high], axis=0),
-        )
-    return total
+    lefts = [masked(parts, j) for j in range(8)]
+    high = jnp.concatenate([l[0] for l in lefts], axis=1)
+    low = jnp.concatenate([l[1] for l in lefts], axis=1)
+    r_high = right_high[...].reshape(2048, 128)
+    r_low = right_low[...].reshape(2048, 128)
+    both = dot(jnp.concatenate([high, low], axis=0), r_high)
+    return both[0:32] + both[32:64] + dot(high, r_low)
 
 
 def mix(r, own, dispatch):
@@ -287,9 +284,10 @@
     y_inverse(r, mixed, r.send1, dispatch)
 
 
-def mix_adjoint(r, own, dispatch):
+def mix_adjoint(r, own, dispatch, share):
     grad_modes = y_forward(r, r.recv2)
     r.g_all[own, :] = grad_modes
+    share()
     back = all_modes(grad_modes, r.bwt_high, r.bwt_low)
     y_inverse(r, back, r.send3, dispatch)
 
@@ -349,7 +347,7 @@
     )
     for i in range(8):
         r.part1[i] = dense[i : i + 1]
-        r.part1[8 + i] = bias_row[i : i + 1]
+    r.part1[8] = bias_row[0:1]
 
 
 def weight_gradient(r):
@@ -394,7 +392,7 @@
 IN_NAMES = ["v", "w", "lw", "bias", "cot", "zf", "xf", "yf", "yi", "xi", "zi"]
 OUT_SHAPES = dict(
     lay=(CELLS, F32), loc=(CELLS, F32), gspec=((2048, 32), F32), recv3=(SLOTS, F32),
-    total=((16, 1, 128), F32), xi=((384, 1024), BF16), zi=((256, 384), BF16),
+    total=((16, 9, 1, 128), F32), xi=((384, 1024), BF16), zi=((256, 384), BF16),
 )
 SCRATCH = dict(
     v=(CELLS, F32), w=((2048, 32), F32), lw=((32, 32), F32), cot=(CELLS, F32),
@@ -405,13 +403,12 @@
     kron_f=((256, 768), BF16), kron_b=((256, 768), BF16),
     flat=((256, 128), F32), spread=((2, 128, 1024), F32),
     s_all=((128, 128), F32), g_all=((128, 128), F32), acc=((256, 256), F32),
-    part1=((16, 1, 128), F32), stage1=((16, 1, 128), F32),
-    part2=((1, 128), F32), stage2=((16, 1, 128), F32), part3=((1, 128), F32),
+    part1=((9, 1, 128), F32), stage1=((16, 9, 1, 128), F32), part2=((9, 1, 128), F32),
     shift=((32, 8, 128), F32),
     send0=(SLOTS, F32), send1=(SLOTS, F32), send2=(SLOTS, F32), send3=(SLOTS, F32),
     recv0=(SLOTS, F32), recv1=(SLOTS, F32), recv2=(SLOTS, F32),
 )
-SEMAPHORES = dict(in_sem=16, send_sem=6, recv_sem=6, small_send=3, small_recv=3)
+SEMAPHORES = dict(in_sem=16, send_sem=6, recv_sem=6, small_send=2, small_recv=2)
 
 
 def kernel(*refs):
@@ -531,46 +528,33 @@
     x_forward(r, r.send2, send_to(r.send2, r.recv2, 2))
 
     point_sums(r)
-    for i, (to_group, to_peer) in enumerate(around):
+    for dy, dx in FAR_FIRST[:-1]:
         pltpu.make_async_remote_copy(
-            src_ref=r.part1.at[to_group * 4 + to_peer % 4],
-            dst_ref=r.stage1.at[spot],
+            src_ref=r.part1,
+            dst_ref=r.stage1.at[me // 4],
             send_sem=r.small_send.at[0],
             recv_sem=r.small_recv.at[0],
+            device_id=(group, peer_of(dy, dx, my_z)),
+            device_id_type=MESH,
+        ).start()
+    r.stage1[me // 4] = r.part1[...]
+    channel_mix(r.kron_b, r.gp, r.loc)
+
+    await_bytes(r.recv2, r.recv_sem.at[2])
+    await_bytes(r.stage1.at[fifteen], r.small_recv.at[0])
+    r.part2[...] = jnp.sum(r.stage1[...], axis=0)
+    for to_group, to_peer in around:
+        pltpu.make_async_remote_copy(
+            src_ref=r.part2,
+            dst_ref=r.total.at[spot],
+            send_sem=r.small_send.at[1],
+            recv_sem=r.small_recv.at[1],
             device_id=(to_group, to_peer),
             device_id_type=MESH,
         ).start()
-    r.stage1[spot] = r.part1[spot]
-    channel_mix(r.kron_b, r.gp, r.loc)
-
-    await_bytes(r.stage1.at[fifteen], r.small_recv.at[0])
-    r.part2[...] = jnp.sum(r.stage1[...], axis=0)
-    for dy, dx in FAR_FIRST[:-1]:
-        pltpu.make_async_remote_copy(
-            src_ref=r.part2,
-            dst_ref=r.stage2.at[me // 4],
-            send_sem=r.small_send.at[1],
-            recv_sem=r.small_recv.at[1],
-            device_id=(group, peer_of(dy, dx, my_z)),
-            device_id_type=MESH,
-        ).start()
-    r.stage2[me // 4] = r.part2[...]
-    await_bytes(r.recv2, r.recv_sem.at[2])
-    mix_adjoint(r, own, send_to(r.send3, r.recv3, 3))
-    share(r.g_all, 5)
-
-    await_bytes(r.stage2.at[fifteen], r.small_recv.at[1])
-    r.part3[...] = jnp.sum(r.stage2[...], axis=0) * (1.0 / math.sqrt(8 * X * Y * Z))
-    for to_group, to_peer in around:
-        pltpu.make_async_remote_copy(
-            src_ref=r.part3,
-            dst_ref=r.total.at[spot],
-            send_sem=r.small_send.at[2],
-            recv_sem=r.small_recv.at[2],
-            device_id=(to_group, to_peer),
-            device_id_type=MESH,
-        ).start()
-    r.total[spot] = r.part3[...]
+    r.total[spot] = r.part2[...]
+    mix_adjoint(r, own, send_to(r.send3, r.recv3, 3), lambda: share(r.g_all, 5))
+
     for buffer, index in ((r.s_all, 4), (r.g_all, 5)):
         await_bytes(buffer.at[pl.ds(0, 96)], r.recv_sem.at[index])
     weight_gradient(r)
@@ -580,9 +564,8 @@
     for index, buffer in ((4, r.s_all), (5, r.g_all)):
         await_bytes(buffer.at[pl.ds(0, 96)], r.send_sem.at[index])
     await_bytes(r.stage1.at[fifteen], r.small_send.at[0])
-    await_bytes(r.stage2.at[fifteen], r.small_send.at[1])
-    await_bytes(r.total.at[fifteen], r.small_send.at[2])
-    await_bytes(r.total.at[fifteen], r.small_recv.at[2])
+    await_bytes(r.total.at[fifteen], r.small_send.at[1])
+    await_bytes(r.total.at[fifteen], r.small_recv.at[1])
     await_bytes(r.recv3, r.recv_sem.at[3])
 
 
@@ -603,7 +586,7 @@
 
     copy(r.lay, r.layer_out)
     copy(r.gspec, r.grad_spectral)
-    total = r.total[...].reshape(16, 128)
+    total = jnp.sum(r.total[...], axis=0).reshape(9, 128) * (1.0 / math.sqrt(8 * X * Y * Z))
     for k in range(4):
         r.grad_local[pl.ds(8 * k, 8), :] = roll(total[0:8], -32 * k)[:, 0:32]
     r.grad_bias[...] = total[8:9, 0:32]

time: 50.9 us -> 50.2 us (0.986)
  Pallas kernels: 50.2 us -> 49.5 us
    pallas_call x1, Pallas kernels: 47.1 us -> 46.4 us  [shards(): pl.pallas_call(kernel, out_shape=tuple((pltpu.VMEM(*s) for s in OUT_SHAPE...]
where the time goes in v2:
time: 50.2 us; the launch traced here: 50.1 us
  Pallas kernels  49.5 us (99%)
  between operations  0.64 us (1%)
    pallas_call x1, Pallas kernels, shards(): pl.pallas_call(kernel, out_shape=tuple((pltpu.VMEM(*s) for s in OUT_SHAPE...  46.4 us
    pallas_call x1, Pallas kernels, shards(): pl.pallas_call(tail, out_shape=(jax.ShapeDtypeStruct(CELLS, F32), jax.Sha...  3.11 us

profile of v2, /device:TPU:1, one launch (start us, length us, event | category | flops | bytes accessed | tf_op | source)
XLA Modules:
  0.0 50.1 jit_solution(3267153406512879666)
XLA Ops:
  0.6 46.4 %fno_layer.1 = (f32[4,32,32,128]{3,2,1,0:T(8,128)S(1)}, f32[4,32,32,128]{3,2,1,0:T(8,128)S(1)}, f32[2048,32]{1,0:T(8,128)S(1)}, f32[64,4,128]{2,1,0:T(4,128)S(1)...) custom-call(f32[4,32,32,128]{3,2,1,0:T(8,128)} %bitcast.11, ...), custom_call_target="tpu_custom_call" | custom-call | tf_op jit(solution)/shard_map/fno_layer/pallas_call | solution.py:613
  47.0 3.1 %fno_tail.1 = (f32[4,32,32,128]{3,2,1,0:T(8,128)}, f32[4,32,32,128]{3,2,1,0:T(8,128)}, f32[2048,32]{1,0:T(8,128)}, f32[32,32]{1,0:T(8,128)}, f32[1,32]{1,0:T(1,128)}) custom-call(f32[4,32,32,128]{3,2,1,0:T(8,128)S(1)} %get-tuple-element.17.refs_0_, f32[4,32,32,128]{3,2,1,0:T(8,128)S(1)} %get-tuple-element.18.refs_1_, ...), custom_call_target="tpu_custom_call" | custom-call | tf_op jit(solution)/shard_map/fno_tail/pallas_call | solution.py:633

commit v3 on v2

--- a/solution.py
+++ b/solution.py
@@ -57,7 +57,7 @@
     xi = np.stack(
         [np.stack([cos_x.T, sin_x.T], 1), np.stack([-sin_x.T, cos_x.T], 1)], 0
     )
-    xi = np.einsum("akbx,mn->maknbx", xi, np.eye(4)).reshape(128, 1024) * scaling
+    xi = np.einsum("akbx,mn->maknbx", xi, np.eye(2)).reshape(64, 512) * scaling
     xi_high, xi_low = halves(xi)
     return (
         left(zf),
@@ -178,16 +178,13 @@
 
 def x_inverse(r, recv):
     r.flat[...] = recv[...].reshape(256, 128)
-    for g in range(2):
+    for g in range(4):
         pieces = []
-        for k4 in range(4):
-            kz = g * 4 + k4
+        for k2 in range(2):
             for ri in range(2):
-                start = (kz // 2) * 4 + ri * 2 + kz % 2
-                pieces.append(r.flat[pl.ds(start, 16, stride=16), :])
-        block = jnp.concatenate(pieces, axis=0)
-        turned = block.T
-        r.spread[g] = dot(lanes_of(turned), r.xi[...])
+                pieces.append(r.flat[pl.ds(g * 4 + ri * 2 + k2, 16, stride=16), :])
+        block = rows_of(jnp.concatenate(pieces, axis=0))
+        r.spread[g // 2, :, g % 2 * 512 : g % 2 * 512 + 512] = dot_tn(block, r.xi[...])
 
 
 def z_inverse(r, t, pair):
@@ -284,10 +281,9 @@
     y_inverse(r, mixed, r.send1, dispatch)
 
 
-def mix_adjoint(r, own, dispatch, share):
+def mix_adjoint(r, own, dispatch):
     grad_modes = y_forward(r, r.recv2)
     r.g_all[own, :] = grad_modes
-    share()
     back = all_modes(grad_modes, r.bwt_high, r.bwt_low)
     y_inverse(r, back, r.send3, dispatch)
 
@@ -391,8 +387,8 @@
 CELLS, SLOTS = (4, 32, 32, 128), (64, 4, 128)
 IN_NAMES = ["v", "w", "lw", "bias", "cot", "zf", "xf", "yf", "yi", "xi", "zi"]
 OUT_SHAPES = dict(
-    lay=(CELLS, F32), loc=(CELLS, F32), gspec=((2048, 32), F32), recv3=(SLOTS, F32),
-    total=((16, 9, 1, 128), F32), xi=((384, 1024), BF16), zi=((256, 384), BF16),
+    lay=(CELLS, F32), loc=(CELLS, F32), s_all=((128, 128), F32), g_all=((128, 128), F32), recv3=(SLOTS, F32),
+    total=((16, 9, 1, 128), F32), xi=((192, 512), BF16), zi=((256, 384), BF16),
 )
 SCRATCH = dict(
     v=(CELLS, F32), w=((2048, 32), F32), lw=((32, 32), F32), cot=(CELLS, F32),
@@ -402,7 +398,7 @@
     bwt_high=((16, 128, 128), BF16), bwt_low=((16, 128, 128), BF16),
     kron_f=((256, 768), BF16), kron_b=((256, 768), BF16),
     flat=((256, 128), F32), spread=((2, 128, 1024), F32),
-    s_all=((128, 128), F32), g_all=((128, 128), F32), acc=((256, 256), F32),
+    acc=((256, 256), F32),
     part1=((9, 1, 128), F32), stage1=((16, 9, 1, 128), F32), part2=((9, 1, 128), F32),
     shift=((32, 8, 128), F32),
     send0=(SLOTS, F32), send1=(SLOTS, F32), send2=(SLOTS, F32), send3=(SLOTS, F32),
@@ -553,11 +549,11 @@
             device_id_type=MESH,
         ).start()
     r.total[spot] = r.part2[...]
-    mix_adjoint(r, own, send_to(r.send3, r.recv3, 3), lambda: share(r.g_all, 5))
+    mix_adjoint(r, own, send_to(r.send3, r.recv3, 3))
+    share(r.g_all, 5)
 
     for buffer, index in ((r.s_all, 4), (r.g_all, 5)):
         await_bytes(buffer.at[pl.ds(0, 96)], r.recv_sem.at[index])
-    weight_gradient(r)
 
     for index, buffer in enumerate((r.send0, r.send1, r.send2, r.send3)):
         await_bytes(buffer, r.send_sem.at[index])
@@ -570,7 +566,7 @@
 
 
 TAIL_SCRATCH = dict(
-    flat=((256, 128), F32), spread=((2, 128, 1024), F32), res=(CELLS, F32),
+    flat=((256, 128), F32), spread=((2, 128, 1024), F32), res=(CELLS, F32), gspec=((2048, 32), F32),
 )
 
 
@@ -585,6 +581,7 @@
         copies[-1].start()
 
     copy(r.lay, r.layer_out)
+    weight_gradient(r)
     copy(r.gspec, r.grad_spectral)
     total = jnp.sum(r.total[...], axis=0).reshape(9, 128) * (1.0 / math.sqrt(8 * X * Y * Z))
     for k in range(4):

time: 50.2 us -> 49.8 us (level)
  no operation moved by 1% of the time
where the time goes in v3:
time: 49.8 us; the launch traced here: 49.7 us
  Pallas kernels  49.1 us (99%)
  between operations  0.64 us (1%)
    pallas_call x1, Pallas kernels, shards(): pl.pallas_call(kernel, out_shape=tuple((pltpu.VMEM(*s) for s in OUT_SHAPE...  46 us
    pallas_call x1, Pallas kernels, shards(): pl.pallas_call(tail, out_shape=(jax.ShapeDtypeStruct(CELLS, F32), jax.Sha...  3.1 us

profile of v3, /device:TPU:1, one launch (start us, length us, event | category | flops | bytes accessed | tf_op | source)
XLA Modules:
  0.0 49.7 jit_solution(3587948546319385027)
XLA Ops:
  0.6 46.0 %fno_layer.1 = (f32[4,32,32,128]{3,2,1,0:T(8,128)S(1)}, f32[4,32,32,128]{3,2,1,0:T(8,128)S(1)}, f32[128,128]{1,0:T(8,128)S(1)}, f32[128,128]{1,0:T(8,128)S(1)}, ...) custom-call(f32[4,32,32,128]{3,2,1,0:T(8,128)} %bitcast.11, ...), custom_call_target="tpu_custom_call" | custom-call | tf_op jit(solution)/shard_map/fno_layer/pallas_call | solution.py:610
  46.6 3.1 %fno_tail.1 = (f32[4,32,32,128]{3,2,1,0:T(8,128)}, f32[4,32,32,128]{3,2,1,0:T(8,128)}, f32[2048,32]{1,0:T(8,128)}, f32[32,32]{1,0:T(8,128)}, f32[1,32]{1,0:T(1,128)}) custom-call(f32[4,32,32,128]{3,2,1,0:T(8,128)S(1)} %get-tuple-element.18.refs_0_, f32[4,32,32,128]{3,2,1,0:T(8,128)S(1)} %get-tuple-element.19.refs_1_, ...), custom_call_target="tpu_custom_call" | custom-call | tf_op jit(solution)/shard_map/fno_tail/pallas_call | solution.py:630

commit v4 on v3

--- a/solution.py
+++ b/solution.py
@@ -281,9 +281,10 @@
     y_inverse(r, mixed, r.send1, dispatch)
 
 
-def mix_adjoint(r, own, dispatch):
+def mix_adjoint(r, own, dispatch, column_sums):
     grad_modes = y_forward(r, r.recv2)
     r.g_all[own, :] = grad_modes
+    column_sums()
     back = all_modes(grad_modes, r.bwt_high, r.bwt_low)
     y_inverse(r, back, r.send3, dispatch)
 
@@ -307,20 +308,16 @@
 
 def point_sums(r):
     same = same_z()
-    r.acc[...] = jnp.zeros((256, 256), F32)
     for t in range(4):
-        for pair in range(2):
-            a_cols, b_cols = [], []
-            for half in range(2):
-                zb = 2 * pair + half
-                a_cols.append(r.v[t, :, pl.ds(zb * 8, 8), :].reshape(256, 128))
-                b_cols.append(r.gp[t, :, pl.ds(zb * 8, 8), :].reshape(256, 128))
-            a_high, a_low = split(jnp.concatenate(a_cols, axis=1))
-            b_high, b_low = split(jnp.concatenate(b_cols, axis=1))
-            r.acc[...] += dot_nt(
-                jnp.concatenate([a_high, a_high, a_low], axis=1),
-                jnp.concatenate([b_high, b_low, b_high], axis=1),
-            )
+        a_cols = [r.v[t, :, pl.ds(zb * 8, 8), :].reshape(256, 128) for zb in range(4)]
+        b_cols = [r.gp[t, :, pl.ds(zb * 8, 8), :].reshape(256, 128) for zb in range(4)]
+        a_high, a_low = split(jnp.concatenate(a_cols, axis=1))
+        b_high, b_low = split(jnp.concatenate(b_cols, axis=1))
+        term = dot_nt(
+            jnp.concatenate([a_high, a_high, a_low], axis=1),
+            jnp.concatenate([b_high, b_low, b_high], axis=1),
+        )
+        r.acc[...] = term if t == 0 else r.acc[...] + term
     folded = jnp.sum(jnp.where(same, r.acc[...], 0.0).reshape(32, 8, 256), axis=1)
     pick = (iota((256, 128), 0) // 8 == iota((256, 128), 1)).astype(F32).astype(BF16)
     fold_high, fold_low = split(folded)
@@ -537,19 +534,22 @@
     channel_mix(r.kron_b, r.gp, r.loc)
 
     await_bytes(r.recv2, r.recv_sem.at[2])
-    await_bytes(r.stage1.at[fifteen], r.small_recv.at[0])
-    r.part2[...] = jnp.sum(r.stage1[...], axis=0)
-    for to_group, to_peer in around:
-        pltpu.make_async_remote_copy(
-            src_ref=r.part2,
-            dst_ref=r.total.at[spot],
-            send_sem=r.small_send.at[1],
-            recv_sem=r.small_recv.at[1],
-            device_id=(to_group, to_peer),
-            device_id_type=MESH,
-        ).start()
-    r.total[spot] = r.part2[...]
-    mix_adjoint(r, own, send_to(r.send3, r.recv3, 3))
+
+    def column_sums():
+        await_bytes(r.stage1.at[fifteen], r.small_recv.at[0])
+        r.part2[...] = jnp.sum(r.stage1[...], axis=0)
+        for to_group, to_peer in around:
+            pltpu.make_async_remote_copy(
+                src_ref=r.part2,
+                dst_ref=r.total.at[spot],
+                send_sem=r.small_send.at[1],
+                recv_sem=r.small_recv.at[1],
+                device_id=(to_group, to_peer),
+                device_id_type=MESH,
+            ).start()
+        r.total[spot] = r.part2[...]
+
+    mix_adjoint(r, own, send_to(r.send3, r.recv3, 3), column_sums)
     share(r.g_all, 5)
 
     for buffer, index in ((r.s_all, 4), (r.g_all, 5)):

time: 49.8 us -> 49.4 us (level)
  Pallas kernels: 49.1 us -> 48.6 us
where the time goes in v4:
time: 49.4 us; the launch traced here: 49.3 us
  Pallas kernels  48.6 us (98%)
  between operations  0.64 us (1%)
    pallas_call x1, Pallas kernels, shards(): pl.pallas_call(kernel, out_shape=tuple((pltpu.VMEM(*s) for s in OUT_SHAPE...  45.5 us
    pallas_call x1, Pallas kernels, shards(): pl.pallas_call(tail, out_shape=(jax.ShapeDtypeStruct(CELLS, F32), jax.Sha...  3.1 us

profile of v4, /device:TPU:1, one launch (start us, length us, event | category | flops | bytes accessed | tf_op | source)
XLA Modules:
  0.0 49.3 jit_solution(3469156597761122733)
XLA Ops:
  0.6 45.5 %fno_layer.1 = (f32[4,32,32,128]{3,2,1,0:T(8,128)S(1)}, f32[4,32,32,128]{3,2,1,0:T(8,128)S(1)}, f32[128,128]{1,0:T(8,128)S(1)}, f32[128,128]{1,0:T(8,128)S(1)}, ...) custom-call(f32[4,32,32,128]{3,2,1,0:T(8,128)} %bitcast.11, ...), custom_call_target="tpu_custom_call" | custom-call | tf_op jit(solution)/shard_map/fno_layer/pallas_call | solution.py:610
  46.2 3.1 %fno_tail.1 = (f32[4,32,32,128]{3,2,1,0:T(8,128)}, f32[4,32,32,128]{3,2,1,0:T(8,128)}, f32[2048,32]{1,0:T(8,128)}, f32[32,32]{1,0:T(8,128)}, f32[1,32]{1,0:T(1,128)}) custom-call(f32[4,32,32,128]{3,2,1,0:T(8,128)S(1)} %get-tuple-element.18.refs_0_, f32[4,32,32,128]{3,2,1,0:T(8,128)S(1)} %get-tuple-element.19.refs_1_, ...), custom_call_target="tpu_custom_call" | custom-call | tf_op jit(solution)/shard_map/fno_tail/pallas_call | solution.py:630
